TPU v7x, 32 devices: a whole 2x2x4 slice. The times are simulated.
32 devices in a mesh: exp: 4 (over z), skyx: 2 (over core), skyy: 4 (over y, x).
Axes of the slice: x: 2, y: 2, z: 4, core: 2. Of those that a mesh axis runs over, the one named last changes fastest.
Arguments:
- estimate: float32 [512, 1024], P('skyx', 'skyy'), may hold values from 0.5 to 102
- observed: float32 [4, 512, 1024], P('exp', 'skyx', 'skyy'), may hold values from 0.25 to 4
- psf_bank: float32 [4, 4, 65, 65], P('exp'), may hold values from 0.1 to 1
- psf_index: int32 [4, 2, 4], P('exp'), may hold values from 0 to 3
- coverage: int32 [4, 2, 4], replicated, may hold values from 0 to 1, as said below
Outputs:
- updated: float32 [512, 1024], P('skyx', 'skyy')
Inputs may be any that keep to these rules, and one draw needn't show every extreme that they name: `coverage`: every tile is covered by at least one exposure.
All inputs are finite; a program needn't handle non-finite values.
Results may differ from a plain program's by a relative error of at most 0.0003.
Values sent between devices are 32-bit elements; how exact they have to be, the bound alone decides.
A program may use at most 64 MiB of HBM per device.

v0:
```python
import functools

import jax
import jax.numpy as jnp
import ml_dtypes
import numpy as np
from jax import lax
from jax.experimental import pallas as pl
from jax.experimental.pallas import tpu as pltpu
from jax.sharding import PartitionSpec as P

MESH = pl.DeviceIdType.MESH
LANES = 128
DIRS = ((0, -1), (0, 1), (-1, 0), (1, 0), (-1, -1), (-1, 1), (1, -1), (1, 1))


def halves(table):
    high = table.astype(ml_dtypes.bfloat16)
    low = (table - high.astype(np.float64)).astype(ml_dtypes.bfloat16)
    return np.stack([high, low])


def make_tables(tile, radius):
    length = tile + 2 * radius
    half = length // 2
    wide = -(-half // LANES) * LANES
    freq = np.arange(half) + 0.5
    center = np.arange(radius, radius + tile)
    places = np.concatenate([center, np.arange(radius), np.arange(radius + tile, length)])
    taps = np.arange(2 * radius + 1) - radius

    def rows(where):
        angle = 2.0 * np.pi / length * np.outer(freq, where)
        return np.concatenate([np.cos(angle), np.sin(angle)])

    def cols(where, depth):
        angle = 2.0 * np.pi / length * np.outer(where, freq)
        table = np.zeros((depth, 2 * wide))
        table[: len(where), :half] = np.cos(angle)
        table[: len(where), wide : wide + half] = np.sin(angle)
        return table

    kern_depth = -(-len(taps) // LANES) * LANES
    kern_rows = np.zeros((length, kern_depth))
    kern_rows[:, : len(taps)] = rows(taps)
    return tuple(
        halves(t)
        for t in (
            cols(places, tile + LANES),
            rows(places),
            cols(center, tile).T.copy(),
            rows(center).T.copy(),
            cols(taps, kern_depth),
            kern_rows,
        )
    )


def split(x):
    high = x.astype(jnp.bfloat16)
    return high, (x - high.astype(jnp.float32)).astype(jnp.bfloat16)


def dot3(a, b):
    def one(x, y):
        return jnp.dot(x, y, preferred_element_type=jnp.float32)

    return one(a[0], b[0]) + (one(a[1], b[0]) + one(a[0], b[1]))


def kernel(
    sizes,
    est_ref, obs_ref, psf_ref, idx_ref, cov_ref,
    h_fc, h_fr, h_ic, h_ir, h_kc, h_kr,
    out_ref,
    t_fc, t_fr, t_ic, t_ir, t_kc, t_kr,
    kpad, kspec, ratio, pack, tb, lr, corner, a_ref, back, slots,
    table_sem, send_sem, recv_sem, rs_send, rs_recv, ag_send, ag_recv,
):
    n_exp, n_x, n_y, radius = sizes
    tile = est_ref.shape[0]
    length = tile + 2 * radius
    half = length // 2
    wide = t_fc.shape[2] // 2
    groups = LANES // radius
    per = tile // groups
    chunk = tile // n_exp
    me = lax.axis_index("exp")
    tx = lax.axis_index("skyx")
    ty = lax.axis_index("skyy")

    def valid(dx, dy):
        x, y = tx + dx, ty + dy
        return (x >= 0) & (x < n_x) & (y >= 0) & (y < n_y)

    def sky(dx, dy):
        return {"skyx": tx + dx, "skyy": ty + dy}

    def peer(d):
        return lax.rem(me + d, n_exp)

    barrier = pltpu.get_barrier_semaphore()
    for dx, dy in DIRS:
        @pl.when(valid(dx, dy))
        def _():
            pl.semaphore_signal(barrier, inc=1, device_id=sky(dx, dy), device_id_type=MESH)
    for d in range(1, n_exp):
        pl.semaphore_signal(barrier, inc=1, device_id={"exp": peer(d)}, device_id_type=MESH)

    loads = [
        pltpu.make_async_copy(source, target, table_sem.at[i])
        for i, (source, target) in enumerate(
            ((h_kc, t_kc), (h_kr, t_kr), (h_fc, t_fc), (h_fr, t_fr), (h_ir, t_ir), (h_ic, t_ic))
        )
    ]
    for load in loads:
        load.start()

    lane = lax.broadcasted_iota(jnp.int32, (per, LANES), 1)
    lane_r = lax.broadcasted_iota(jnp.int32, (radius, LANES), 1)

    def pack_sides(source, turn):
        left = jnp.zeros((per, LANES), jnp.float32)
        right = jnp.zeros((per, LANES), jnp.float32)
        for g in range(groups):
            here = (lane >= g * radius) & (lane < (g + 1) * radius)
            low = source[g * per : (g + 1) * per, 0:LANES]
            high = source[g * per : (g + 1) * per, tile - LANES : tile]
            shift = g * radius
            left = jnp.where(here, pltpu.roll(low, shift, 1) if shift else low, left)
            shift = (g * radius + radius) % LANES
            right = jnp.where(here, pltpu.roll(high, shift, 1) if shift else high, right)
        pack[turn, 0] = left
        pack[turn, 1] = right

    def copies(source, turn):
        ends = (
            (pack.at[turn, 0], lr.at[turn, 1]),
            (pack.at[turn, 1], lr.at[turn, 0]),
            (source.at[0:radius], tb.at[turn, radius : 2 * radius]),
            (source.at[tile - radius : tile], tb.at[turn, 0:radius]),
            (pack.at[turn, 0, 0:radius], corner.at[turn, 3]),
            (pack.at[turn, 1, 0:radius], corner.at[turn, 2]),
            (pack.at[turn, 0, per - radius : per], corner.at[turn, 1]),
            (pack.at[turn, 1, per - radius : per], corner.at[turn, 0]),
        )
        made = []
        for k, ((dx, dy), (src, dst)) in enumerate(zip(DIRS, ends)):
            out = pltpu.make_async_remote_copy(
                src_ref=src, dst_ref=dst, send_sem=send_sem.at[turn, k],
                recv_sem=recv_sem.at[turn, k], device_id=sky(dx, dy), device_id_type=MESH,
            )
            made.append((out, valid(dx, dy), valid(-dx, -dy), dst))
        return made

    def start(made):
        for out, sends, receives, dst in made:
            @pl.when(sends)
            def _():
                out.start()

            @pl.when(jnp.logical_not(receives))
            def _():
                dst[...] = jnp.zeros(dst.shape, jnp.float32)

    def arrive(made):
        for out, sends, receives, dst in made:
            @pl.when(receives)
            def _():
                out.wait_recv()

    def finish(made):
        for out, sends, receives, dst in made:
            @pl.when(sends)
            def _():
                out.wait_send()

    def pair(table, *where):
        return table[(0,) + where], table[(1,) + where]

    every = slice(None)

    def begin(center):
        a_ref[...] = dot3(split(center), pair(t_fc, slice(0, tile), every))

    def sides(turn):
        left, right = lr[turn, 0], lr[turn, 1]
        parts = []
        for g in range(groups):
            shift = (-g * radius) % LANES
            low = pltpu.roll(left, shift, 1) if shift else left
            shift = (radius - g * radius) % LANES
            high = pltpu.roll(right, shift, 1) if shift else right
            parts.append(jnp.where(lane < radius, low, jnp.where(lane < 2 * radius, high, 0.0)))
        return jnp.concatenate(parts, axis=0)

    def corners(turn):
        def row(low, high):
            return jnp.where(
                lane_r < radius, low, jnp.where(lane_r < 2 * radius, high, 0.0)
            )

        top = row(
            pltpu.roll(corner[turn, 0], radius, 1), pltpu.roll(corner[turn, 1], 2 * radius, 1)
        )
        bottom = row(corner[turn, 2], pltpu.roll(corner[turn, 3], radius, 1))
        return jnp.concatenate([top, bottom], axis=0)

    def spectrum(turn):
        outer = pair(t_fc, slice(tile, tile + LANES), every)
        inner = pair(t_fc, slice(0, tile), every)
        mid = split(a_ref[...] + dot3(split(sides(turn)), outer))
        edge = split(dot3(split(tb[turn]), inner) + dot3(split(corners(turn)), outer))
        return dot3(pair(t_fr, every, slice(0, tile)), mid) + dot3(
            pair(t_fr, every, slice(tile, length)), edge
        )

    def combos(z):
        p, q = z[0:half, 0:wide], z[0:half, wide:]
        r, t = z[half:, 0:wide], z[half:, wide:]
        return p - t, r + q, p + t, r - q

    def mix(z, sign):
        u, v, e, d = combos(z)
        ku, kv, ke, kd = kspec[0], kspec[1], kspec[2], kspec[3]
        u2 = u * ku - sign * (v * kv)
        v2 = v * ku + sign * (u * kv)
        e2 = e * ke - sign * (d * kd)
        d2 = d * ke + sign * (e * kd)
        top = jnp.concatenate([u2 + e2, v2 - d2], axis=1)
        bottom = jnp.concatenate([v2 + d2, e2 - u2], axis=1)
        return jnp.concatenate([top, bottom], axis=0)

    def field(z):
        left = dot3(pair(t_ir, every, every), split(z))
        return dot3(split(left), pair(t_ic, every, every))

    pack_sides(est_ref, 0)

    neighbours = n_exp - 1
    for dx, dy in DIRS:
        neighbours = neighbours + valid(dx, dy).astype(jnp.int32)
    pl.semaphore_wait(barrier, neighbours)

    first = copies(est_ref, 0)
    start(first)

    side = psf_ref.shape[-1]
    kpad[...] = jnp.zeros(kpad.shape, jnp.float32)
    kpad[0:side, 0:side] = psf_ref[0, idx_ref[0, tx, ty]]
    at_row = lax.broadcasted_iota(jnp.int32, kpad.shape, 0).astype(jnp.float32) - radius
    at_col = lax.broadcasted_iota(jnp.int32, kpad.shape, 1).astype(jnp.float32) - radius
    envelope = jnp.exp(-(at_row * at_row + at_col * at_col) / (2.0 * (0.625 * radius) ** 2))
    raw = kpad[...] * envelope
    scaled = raw / jnp.sum(raw) * (1.0 / (2.0 * half * half))
    loads[0].wait()
    loads[1].wait()
    k_cols = dot3(split(scaled), pair(t_kc, every, every))
    k_all = dot3(pair(t_kr, every, every), split(k_cols))
    for i, part in enumerate(combos(k_all)):
        kspec[i] = part

    loads[2].wait()
    begin(est_ref[...])
    loads[3].wait()
    loads[4].wait()
    loads[5].wait()

    covering = jnp.float32(0.0)
    for e in range(n_exp):
        covering = covering + cov_ref[e, tx, ty].astype(jnp.float32)
    mine = cov_ref[me, tx, ty].astype(jnp.float32)

    arrive(first)
    blurred = field(mix(spectrum(0), 1.0))
    ratio[...] = mine * obs_ref[0] / blurred
    pack_sides(ratio, 1)
    second = copies(ratio, 1)
    start(second)
    begin(ratio[...])
    arrive(second)
    back[...] = mine * field(mix(spectrum(1), -1.0))

    def block(index):
        return pl.ds(pl.multiple_of(index * chunk, chunk), chunk)

    scatter = []
    for d in range(1, n_exp):
        out = pltpu.make_async_remote_copy(
            src_ref=back.at[block(peer(d))], dst_ref=slots.at[d - 1],
            send_sem=rs_send.at[d - 1], recv_sem=rs_recv.at[d - 1],
            device_id={"exp": peer(d)}, device_id_type=MESH,
        )
        out.start()
        scatter.append(out)
    total = back[block(me), :]
    for d in range(1, n_exp):
        scatter[d - 1].wait_recv()
        total = total + slots[d - 1]
    out_ref[block(me), :] = est_ref[block(me), :] * total / covering
    gather = []
    for d in range(1, n_exp):
        out = pltpu.make_async_remote_copy(
            src_ref=out_ref.at[block(me)], dst_ref=out_ref.at[block(me)],
            send_sem=ag_send.at[d - 1], recv_sem=ag_recv.at[d - 1],
            device_id={"exp": peer(d)}, device_id_type=MESH,
        )
        out.start()
        gather.append(out)
    for d in range(1, n_exp):
        source = peer(n_exp - d)
        pltpu.make_async_remote_copy(
            src_ref=out_ref.at[block(source)], dst_ref=out_ref.at[block(source)],
            send_sem=ag_send.at[d - 1], recv_sem=ag_recv.at[d - 1],
            device_id={"exp": source}, device_id_type=MESH,
        ).wait_recv()
    finish(first)
    finish(second)
    for out in scatter + gather:
        out.wait_send()


def shards(sizes, estimate, observed, psf_bank, psf_index, coverage):
    tile = estimate.shape[0]
    n_exp, n_x, n_y = sizes
    radius = (psf_bank.shape[-1] - 1) // 2
    tables = make_tables(tile, radius)
    length = tile + 2 * radius
    wide = tables[0].shape[2] // 2
    per = tile * radius // LANES
    kern_depth = tables[4].shape[1]
    f32 = jnp.float32
    vmem = pl.BlockSpec(memory_space=pltpu.VMEM)
    smem = pl.BlockSpec(memory_space=pltpu.SMEM)
    hbm = pl.BlockSpec(memory_space=pl.ANY)
    scratch = [pltpu.VMEM(t.shape, jnp.bfloat16) for t in tables] + [
        pltpu.VMEM((kern_depth, kern_depth), f32),
        pltpu.VMEM((4, length // 2, wide), f32),
        pltpu.VMEM((tile, tile), f32),
        pltpu.VMEM((2, 2, per, LANES), f32),
        pltpu.VMEM((2, 2 * radius, tile), f32),
        pltpu.VMEM((2, 2, per, LANES), f32),
        pltpu.VMEM((2, 4, radius, LANES), f32),
        pltpu.VMEM((tile, 2 * wide), f32),
        pltpu.VMEM((tile, tile), f32),
        pltpu.VMEM((max(n_exp - 1, 1), tile // n_exp, tile), f32),
        pltpu.SemaphoreType.DMA((len(tables),)),
        pltpu.SemaphoreType.DMA((2, len(DIRS))),
        pltpu.SemaphoreType.DMA((2, len(DIRS))),
    ] + [pltpu.SemaphoreType.DMA((max(n_exp - 1, 1),))] * 4
    return pl.pallas_call(
        functools.partial(kernel, (n_exp, n_x, n_y, radius)),
        out_shape=jax.ShapeDtypeStruct((tile, tile), f32),
        in_specs=[vmem, vmem, vmem, smem, smem] + [hbm] * len(tables),
        out_specs=vmem,
        scratch_shapes=scratch,
        compiler_params=pltpu.CompilerParams(
            collective_id=0, has_side_effects=True, vmem_limit_bytes=48 * 1024 * 1024
        ),
    )(estimate, observed, psf_bank, psf_index, coverage, *[jnp.asarray(t) for t in tables])


def solution(mesh):
    in_specs = (
        P("skyx", "skyy"),
        P("exp", "skyx", "skyy"),
        P("exp", None, None, None),
        P("exp", None, None),
        P(),
    )
    sizes = tuple(mesh.shape[name] for name in ("exp", "skyx", "skyy"))
    return jax.shard_map(
        functools.partial(shards, sizes),
        mesh=mesh, in_specs=in_specs, out_specs=P("skyx", "skyy"), check_vma=False,
    )
```

profile of v0, /device:TPU:0, one launch (start us, length us, event | category | flops | bytes accessed | tf_op | source)
XLA Modules:
  0.0 40.7 jit_solution(10731033429412465474)
XLA Ops:
  0.0 0.0 copy-start.8
  0.0 0.0 copy-start.9
  0.0 0.0 copy-start.4
  0.0 1.0 %copy.12.psf_ref = f32[1,4,65,65]{3,2,1,0:T(8,128)S(1)} copy(f32[1,4,65,65]{3,1,2,0:T(4,128)} %param.13) | data formatting | bytes 135200 | tf_op args[2]
  1.0 0.0 copy-done.8
  1.0 0.0 copy-done.9
  1.0 0.1 copy-done.4
  1.0 0.0 copy-start
  1.0 1.1 %copy-done = bf16[2,384,512]{2,1,0:T(8,128)(2,1)S(1)} copy-done((bf16[2,384,512]{2,1,0:T(8,128)(2,1)S(1)}, bf16[2,384,512]{2,1,0:T(8,128)(2,1)}, u32[]{:S(2)}) %copy-start) | copy-done | bytes 786456
  2.2 0.0 copy-start.1
  2.2 1.0 %copy-done.1 = bf16[2,512,256]{2,1,0:T(8,128)(2,1)S(1)} copy-done((bf16[2,512,256]{2,1,0:T(8,128)(2,1)S(1)}, bf16[2,512,256]{2,1,0:T(8,128)(2,1)}, u32[]{:S(2)}) %copy-start.1) | copy-done | bytes 524312
  3.2 0.0 copy-start.2
  3.2 1.0 %copy-done.2 = bf16[2,320,320]{2,1,0:T(8,128)(2,1)S(1)} copy-done((bf16[2,320,320]{2,1,0:T(8,128)(2,1)S(1)}, bf16[2,320,320]{2,1,0:T(8,128)(2,1)}, u32[]{:S(2)}) %copy-start.2) | copy-done | bytes 409624
  4.3 0.0 copy-start.3
  4.3 1.0 %copy-done.3 = bf16[2,256,320]{2,1,0:T(8,128)(2,1)S(1)} copy-done((bf16[2,256,320]{2,1,0:T(8,128)(2,1)S(1)}, bf16[2,256,320]{2,1,0:T(8,128)(2,1)}, u32[]{:S(2)}) %copy-start.3) | copy-done | bytes 327704
  5.2 0.0 copy-start.5
  5.3 0.9 %copy-done.5 = f32[1,256,256]{2,1,0:T(8,128)S(1)} copy-done((f32[1,256,256]{2,1,0:T(8,128)S(1)}, f32[1,256,256]{2,1,0:T(8,128)}, u32[]{:S(2)}) %copy-start.5) | copy-done | bytes 262168
  6.2 0.0 copy-start.6
  6.2 0.9 %copy-done.6 = bf16[2,128,512]{2,1,0:T(8,128)(2,1)S(1)} copy-done((bf16[2,128,512]{2,1,0:T(8,128)(2,1)S(1)}, bf16[2,128,512]{2,1,0:T(8,128)(2,1)}, u32[]{:S(2)}) %copy-start.6) | copy-done | bytes 262168
  7.2 0.0 copy-start.7
  7.2 0.9 %copy-done.7 = bf16[2,320,128]{2,1,0:T(8,128)(2,1)S(1)} copy-done((bf16[2,320,128]{2,1,0:T(8,128)(2,1)S(1)}, bf16[2,320,128]{2,1,0:T(8,128)(2,1)}, u32[]{:S(2)}) %copy-start.7) | copy-done | bytes 163864
  8.1 31.9 %shard_map.109 = f32[256,256]{1,0:T(8,128)S(1)} custom-call(f32[256,256]{1,0:T(8,128)S(1)} %copy-done.4, f32[1,256,256]{2,1,0:T(8,128)S(1)} %copy-done.5, f32[1,4,65,65]{3,2,1,0:T(8,128)S(1)} %copy.12.psf_ref, s32[1,2,4]{2,1,0:T(2,128)S(1)} %copy-done.9, s32[4,2,4]{2,1,0:T(2,128)S(1)} %copy-done.8, bf16[2,384,512]{2,1,0:T(8,128)(2,1)S(1)} %copy-done, ...), custom_call_target="tpu_custom_call" | custom-call | tf_op jit(solution)/shard_map/pallas_call | solution.py:351
  40.0 0.7 %copy.14 = f32[256,256]{1,0:T(8,128)} copy(f32[256,256]{1,0:T(8,128)S(1)} %shard_map.109) | data formatting | bytes 524288
Async XLA Ops:
  0.0 1.0 %copy-start.8 = (s32[4,2,4]{2,1,0:T(2,128)S(1)}, s32[4,2,4]{2,1,0:T(2,128)}, u32[]{:S(2)}) copy-start(s32[4,2,4]{2,1,0:T(2,128)} %cov_ref.1) | copy-start | bytes 388
  0.0 1.0 %copy-start.9 = (s32[1,2,4]{2,1,0:T(2,128)S(1)}, s32[1,2,4]{2,1,0:T(2,128)}, u32[]{:S(2)}) copy-start(s32[1,2,4]{2,1,0:T(2,128)} %idx_ref.1) | copy-start | bytes 100
  0.0 1.0 %copy-start.4 = (f32[256,256]{1,0:T(8,128)S(1)}, f32[256,256]{1,0:T(8,128)}, u32[]{:S(2)}) copy-start(f32[256,256]{1,0:T(8,128)} %est_ref.1) | copy-start | bytes 786436
  1.0 1.1 %copy-start = (bf16[2,384,512]{2,1,0:T(8,128)(2,1)S(1)}, bf16[2,384,512]{2,1,0:T(8,128)(2,1)}, u32[]{:S(2)}) copy-start(bf16[2,384,512]{2,1,0:T(8,128)(2,1)} %constant.12.clone.h_fc) | copy-start | bytes 2359300
  2.2 1.0 %copy-start.1 = (bf16[2,512,256]{2,1,0:T(8,128)(2,1)S(1)}, bf16[2,512,256]{2,1,0:T(8,128)(2,1)}, u32[]{:S(2)}) copy-start(bf16[2,512,256]{2,1,0:T(8,128)(2,1)} %constant.14.clone.h_ic) | copy-start | bytes 1572868
  3.2 1.0 %copy-start.2 = (bf16[2,320,320]{2,1,0:T(8,128)(2,1)S(1)}, bf16[2,320,320]{2,1,0:T(8,128)(2,1)}, u32[]{:S(2)}) copy-start(bf16[2,320,320]{2,1,0:T(8,128)(2,1)} %constant.13.clone.h_fr) | copy-start | bytes 1228804
  4.3 1.0 %copy-start.3 = (bf16[2,256,320]{2,1,0:T(8,128)(2,1)S(1)}, bf16[2,256,320]{2,1,0:T(8,128)(2,1)}, u32[]{:S(2)}) copy-start(bf16[2,256,320]{2,1,0:T(8,128)(2,1)} %constant.15.clone.h_ir) | copy-start | bytes 983044
  5.2 0.9 %copy-start.5 = (f32[1,256,256]{2,1,0:T(8,128)S(1)}, f32[1,256,256]{2,1,0:T(8,128)}, u32[]{:S(2)}) copy-start(f32[1,256,256]{2,1,0:T(8,128)} %obs_ref.1) | copy-start | bytes 786436
  6.2 0.9 %copy-start.6 = (bf16[2,128,512]{2,1,0:T(8,128)(2,1)S(1)}, bf16[2,128,512]{2,1,0:T(8,128)(2,1)}, u32[]{:S(2)}) copy-start(bf16[2,128,512]{2,1,0:T(8,128)(2,1)} %constant.16.clone.h_kc) | copy-start | bytes 786436
  7.2 0.9 %copy-start.7 = (bf16[2,320,128]{2,1,0:T(8,128)(2,1)S(1)}, bf16[2,320,128]{2,1,0:T(8,128)(2,1)}, u32[]{:S(2)}) copy-start(bf16[2,320,128]{2,1,0:T(8,128)(2,1)} %constant.17.clone.h_kr) | copy-start | bytes 491524
where the time goes:
time: 41.1 us; the launch traced here: 40.7 us
  Pallas kernels  31.9 us (78%)
  local copies, waits for them, and re-layouts  8.74 us (21%)
    pallas_call x1, Pallas kernels, shards(): pl.pallas_call(functools.partial(kernel, (n_exp, n_x, n_y, radius)), out_...  31.9 us
    unnamed x22, local copies, waits for them, and re-layouts  8.74 us

commit v1 on v0

--- a/solution.py
+++ b/solution.py
@@ -70,11 +70,11 @@
 
 def kernel(
     sizes,
-    est_ref, obs_ref, psf_ref, idx_ref, cov_ref,
+    h_est, h_obs, h_psf, idx_ref, cov_ref,
     h_fc, h_fr, h_ic, h_ir, h_kc, h_kr,
     out_ref,
-    t_fc, t_fr, t_ic, t_ir, t_kc, t_kr,
-    kpad, kspec, ratio, pack, tb, lr, corner, a_ref, back, slots,
+    t_fc, t_fr, t_ic, t_ir, t_kc, t_kr, est_ref, obs_ref, psf_ref,
+    kpad, kspec, ratio, pack, cpack, tb, lr, corner, a_ref, back, slots,
     table_sem, send_sem, recv_sem, rs_send, rs_recv, ag_send, ag_recv,
 ):
     n_exp, n_x, n_y, radius = sizes
@@ -99,6 +99,18 @@
     def peer(d):
         return lax.rem(me + d, n_exp)
 
+    loads = [
+        pltpu.make_async_copy(source, target, table_sem.at[i])
+        for i, (source, target) in enumerate(
+            (
+                (h_est, est_ref), (h_psf, psf_ref), (h_kc, t_kc), (h_kr, t_kr), (h_fc, t_fc),
+                (h_fr, t_fr), (h_ir, t_ir), (h_ic, t_ic), (h_obs, obs_ref),
+            )
+        )
+    ]
+    for load in loads:
+        load.start()
+
     barrier = pltpu.get_barrier_semaphore()
     for dx, dy in DIRS:
         @pl.when(valid(dx, dy))
@@ -107,17 +119,9 @@
     for d in range(1, n_exp):
         pl.semaphore_signal(barrier, inc=1, device_id={"exp": peer(d)}, device_id_type=MESH)
 
-    loads = [
-        pltpu.make_async_copy(source, target, table_sem.at[i])
-        for i, (source, target) in enumerate(
-            ((h_kc, t_kc), (h_kr, t_kr), (h_fc, t_fc), (h_fr, t_fr), (h_ir, t_ir), (h_ic, t_ic))
-        )
-    ]
-    for load in loads:
-        load.start()
-
     lane = lax.broadcasted_iota(jnp.int32, (per, LANES), 1)
-    lane_r = lax.broadcasted_iota(jnp.int32, (radius, LANES), 1)
+    part = radius // groups
+    lane_c = lax.broadcasted_iota(jnp.int32, (part, LANES), 1)
 
     def pack_sides(source, turn):
         left = jnp.zeros((per, LANES), jnp.float32)
@@ -132,6 +136,22 @@
             right = jnp.where(here, pltpu.roll(high, shift, 1) if shift else high, right)
         pack[turn, 0] = left
         pack[turn, 1] = right
+        for k, block in enumerate(
+            (
+                left[per - radius : per],
+                right[per - radius : per],
+                left[0:radius],
+                right[0:radius],
+            )
+        ):
+            start_lane = (LANES - radius) if k < 2 else 0
+            small = jnp.zeros((part, LANES), jnp.float32)
+            for g in range(groups):
+                here = (lane_c >= g * radius) & (lane_c < (g + 1) * radius)
+                shift = (g * radius - start_lane) % LANES
+                piece = block[g * part : (g + 1) * part]
+                small = jnp.where(here, pltpu.roll(piece, shift, 1) if shift else piece, small)
+            cpack[turn, k] = small
 
     def copies(source, turn):
         ends = (
@@ -139,10 +159,10 @@
             (pack.at[turn, 1], lr.at[turn, 0]),
             (source.at[0:radius], tb.at[turn, radius : 2 * radius]),
             (source.at[tile - radius : tile], tb.at[turn, 0:radius]),
-            (pack.at[turn, 0, 0:radius], corner.at[turn, 3]),
-            (pack.at[turn, 1, 0:radius], corner.at[turn, 2]),
-            (pack.at[turn, 0, per - radius : per], corner.at[turn, 1]),
-            (pack.at[turn, 1, per - radius : per], corner.at[turn, 0]),
+            (cpack.at[turn, 2], corner.at[turn, 3]),
+            (cpack.at[turn, 3], corner.at[turn, 2]),
+            (cpack.at[turn, 0], corner.at[turn, 1]),
+            (cpack.at[turn, 1], corner.at[turn, 0]),
         )
         made = []
         for k, ((dx, dy), (src, dst)) in enumerate(zip(DIRS, ends)):
@@ -195,16 +215,17 @@
         return jnp.concatenate(parts, axis=0)
 
     def corners(turn):
-        def row(low, high):
-            return jnp.where(
-                lane_r < radius, low, jnp.where(lane_r < 2 * radius, high, 0.0)
-            )
-
-        top = row(
-            pltpu.roll(corner[turn, 0], radius, 1), pltpu.roll(corner[turn, 1], 2 * radius, 1)
-        )
-        bottom = row(corner[turn, 2], pltpu.roll(corner[turn, 3], radius, 1))
-        return jnp.concatenate([top, bottom], axis=0)
+        parts = []
+        for low, high in ((corner[turn, 0], corner[turn, 1]), (corner[turn, 2], corner[turn, 3])):
+            for g in range(groups):
+                shift = (-g * radius) % LANES
+                near = pltpu.roll(low, shift, 1) if shift else low
+                shift = (radius - g * radius) % LANES
+                far = pltpu.roll(high, shift, 1) if shift else high
+                parts.append(
+                    jnp.where(lane_c < radius, near, jnp.where(lane_c < 2 * radius, far, 0.0))
+                )
+        return jnp.concatenate(parts, axis=0)
 
     def spectrum(turn):
         outer = pair(t_fc, slice(tile, tile + LANES), every)
@@ -235,6 +256,7 @@
         left = dot3(pair(t_ir, every, every), split(z))
         return dot3(split(left), pair(t_ic, every, every))
 
+    loads[0].wait()
     pack_sides(est_ref, 0)
 
     neighbours = n_exp - 1
@@ -247,24 +269,28 @@
 
     side = psf_ref.shape[-1]
     kpad[...] = jnp.zeros(kpad.shape, jnp.float32)
-    kpad[0:side, 0:side] = psf_ref[0, idx_ref[0, tx, ty]]
+    loads[1].wait()
+    model = idx_ref[0, tx, ty]
+    chosen = psf_ref[0, :, 0, :]
+    for m in range(1, psf_ref.shape[2]):
+        chosen = jnp.where(model == m, psf_ref[0, :, m, :], chosen)
+    kpad[0:side, 0:side] = chosen
     at_row = lax.broadcasted_iota(jnp.int32, kpad.shape, 0).astype(jnp.float32) - radius
     at_col = lax.broadcasted_iota(jnp.int32, kpad.shape, 1).astype(jnp.float32) - radius
     envelope = jnp.exp(-(at_row * at_row + at_col * at_col) / (2.0 * (0.625 * radius) ** 2))
     raw = kpad[...] * envelope
     scaled = raw / jnp.sum(raw) * (1.0 / (2.0 * half * half))
-    loads[0].wait()
-    loads[1].wait()
+    loads[2].wait()
+    loads[3].wait()
     k_cols = dot3(split(scaled), pair(t_kc, every, every))
     k_all = dot3(pair(t_kr, every, every), split(k_cols))
-    for i, part in enumerate(combos(k_all)):
-        kspec[i] = part
-
-    loads[2].wait()
+    for i, term in enumerate(combos(k_all)):
+        kspec[i] = term
+
+    loads[4].wait()
     begin(est_ref[...])
-    loads[3].wait()
-    loads[4].wait()
-    loads[5].wait()
+    for load in loads[5:]:
+        load.wait()
 
     covering = jnp.float32(0.0)
     for e in range(n_exp):
@@ -323,6 +349,7 @@
 def shards(sizes, estimate, observed, psf_bank, psf_index, coverage):
     tile = estimate.shape[0]
     n_exp, n_x, n_y = sizes
+    bank = jnp.transpose(psf_bank, (0, 2, 1, 3))
     radius = (psf_bank.shape[-1] - 1) // 2
     tables = make_tables(tile, radius)
     length = tile + 2 * radius
@@ -332,32 +359,36 @@
     f32 = jnp.float32
     vmem = pl.BlockSpec(memory_space=pltpu.VMEM)
     smem = pl.BlockSpec(memory_space=pltpu.SMEM)
-    hbm = pl.BlockSpec(memory_space=pl.ANY)
+    hbm = pl.BlockSpec(memory_space=pltpu.HBM)
     scratch = [pltpu.VMEM(t.shape, jnp.bfloat16) for t in tables] + [
+        pltpu.VMEM(estimate.shape, f32),
+        pltpu.VMEM(observed.shape, f32),
+        pltpu.VMEM(bank.shape, f32),
         pltpu.VMEM((kern_depth, kern_depth), f32),
         pltpu.VMEM((4, length // 2, wide), f32),
         pltpu.VMEM((tile, tile), f32),
         pltpu.VMEM((2, 2, per, LANES), f32),
+        pltpu.VMEM((2, 4, radius * radius // LANES, LANES), f32),
         pltpu.VMEM((2, 2 * radius, tile), f32),
         pltpu.VMEM((2, 2, per, LANES), f32),
-        pltpu.VMEM((2, 4, radius, LANES), f32),
+        pltpu.VMEM((2, 4, radius * radius // LANES, LANES), f32),
         pltpu.VMEM((tile, 2 * wide), f32),
         pltpu.VMEM((tile, tile), f32),
         pltpu.VMEM((max(n_exp - 1, 1), tile // n_exp, tile), f32),
-        pltpu.SemaphoreType.DMA((len(tables),)),
+        pltpu.SemaphoreType.DMA((len(tables) + 3,)),
         pltpu.SemaphoreType.DMA((2, len(DIRS))),
         pltpu.SemaphoreType.DMA((2, len(DIRS))),
     ] + [pltpu.SemaphoreType.DMA((max(n_exp - 1, 1),))] * 4
     return pl.pallas_call(
         functools.partial(kernel, (n_exp, n_x, n_y, radius)),
         out_shape=jax.ShapeDtypeStruct((tile, tile), f32),
-        in_specs=[vmem, vmem, vmem, smem, smem] + [hbm] * len(tables),
+        in_specs=[hbm, hbm, hbm, smem, smem] + [hbm] * len(tables),
         out_specs=vmem,
         scratch_shapes=scratch,
         compiler_params=pltpu.CompilerParams(
-            collective_id=0, has_side_effects=True, vmem_limit_bytes=48 * 1024 * 1024
+            collective_id=0, has_side_effects=True, vmem_limit_bytes=63 * 1024 * 1024
         ),
-    )(estimate, observed, psf_bank, psf_index, coverage, *[jnp.asarray(t) for t in tables])
+    )(estimate, observed, bank, psf_index, coverage, *[jnp.asarray(t) for t in tables])
 
 
 def solution(mesh):

time: 41.1 us -> 34.1 us (0.83)
  local copies, waits for them, and re-layouts: 8.74 us -> 1.67 us
    unnamed x22 -> x1, local copies, waits for them, and re-layouts: 8.74 us -> 1.67 us
where the time goes in v1:
time: 34.1 us; the launch traced here: 33.9 us
  Pallas kernels  32.3 us (95%)
  local copies, waits for them, and re-layouts  1.67 us (5%)
    pallas_call x1, Pallas kernels, shards(): pl.pallas_call(functools.partial(kernel, (n_exp, n_x, n_y, radius)), out_...  32.3 us
    unnamed x1, local copies, waits for them, and re-layouts  1.67 us

profile of v1, /device:TPU:0, one launch (start us, length us, event | category | flops | bytes accessed | tf_op | source)
XLA Modules:
  0.0 33.9 jit_solution(16393180844776101907)
XLA Ops:
  0.0 32.3 %shard_map.109 = f32[256,256]{1,0:T(8,128)} custom-call(f32[256,256]{1,0:T(8,128)} %h_est.1, f32[1,256,256]{2,1,0:T(8,128)} %h_obs.1, f32[1,65,4,65]{3,2,1,0:T(4,128)} %bitcast.1, s32[1,2,4]{2,1,0:T(2,128)} %idx_ref.1, s32[4,2,4]{2,1,0:T(2,128)} %cov_ref.1, bf16[2,384,512]{2,1,0:T(8,128)(2,1)} %constant.12.clone.h_fc, ...), custom_call_target="tpu_custom_call" | custom-call | tf_op jit(solution)/shard_map/pallas_call | solution.py:382
  32.3 1.7 %copy.13 = f32[256,256]{1,0:T(8,128)} copy(f32[256,256]{1,0:T(8,128)} %shard_map.109) | data formatting | bytes 524288

commit v2 on v1

--- a/solution.py
+++ b/solution.py
@@ -11,6 +11,7 @@
 
 MESH = pl.DeviceIdType.MESH
 LANES = 128
+PIECES = 2
 DIRS = ((0, -1), (0, 1), (-1, 0), (1, 0), (-1, -1), (-1, 1), (1, -1), (1, 1))
 
 
@@ -307,42 +308,51 @@
     arrive(second)
     back[...] = mine * field(mix(spectrum(1), -1.0))
 
-    def block(index):
-        return pl.ds(pl.multiple_of(index * chunk, chunk), chunk)
-
-    scatter = []
-    for d in range(1, n_exp):
-        out = pltpu.make_async_remote_copy(
-            src_ref=back.at[block(peer(d))], dst_ref=slots.at[d - 1],
-            send_sem=rs_send.at[d - 1], recv_sem=rs_recv.at[d - 1],
-            device_id={"exp": peer(d)}, device_id_type=MESH,
-        )
-        out.start()
-        scatter.append(out)
-    total = back[block(me), :]
-    for d in range(1, n_exp):
-        scatter[d - 1].wait_recv()
-        total = total + slots[d - 1]
-    out_ref[block(me), :] = est_ref[block(me), :] * total / covering
+    piece = chunk // PIECES
+
+    def block(index, k):
+        return pl.ds(pl.multiple_of(index * chunk + k * piece, piece), piece)
+
+    scatter = {}
+    for k in range(PIECES):
+        for d in range(1, n_exp):
+            at = (d - 1) * PIECES + k
+            out = pltpu.make_async_remote_copy(
+                src_ref=back.at[block(peer(d), k)], dst_ref=slots.at[at],
+                send_sem=rs_send.at[at], recv_sem=rs_recv.at[at],
+                device_id={"exp": peer(d)}, device_id_type=MESH,
+            )
+            out.start()
+            scatter[d, k] = out
     gather = []
-    for d in range(1, n_exp):
-        out = pltpu.make_async_remote_copy(
-            src_ref=out_ref.at[block(me)], dst_ref=out_ref.at[block(me)],
-            send_sem=ag_send.at[d - 1], recv_sem=ag_recv.at[d - 1],
-            device_id={"exp": peer(d)}, device_id_type=MESH,
-        )
-        out.start()
-        gather.append(out)
-    for d in range(1, n_exp):
-        source = peer(n_exp - d)
-        pltpu.make_async_remote_copy(
-            src_ref=out_ref.at[block(source)], dst_ref=out_ref.at[block(source)],
-            send_sem=ag_send.at[d - 1], recv_sem=ag_recv.at[d - 1],
-            device_id={"exp": source}, device_id_type=MESH,
-        ).wait_recv()
+    for k in range(PIECES):
+        here = block(me, k)
+        total = back[here, :]
+        for d in range(1, n_exp):
+            scatter[d, k].wait_recv()
+            total = total + slots[(d - 1) * PIECES + k]
+        out_ref[here, :] = est_ref[here, :] * total / covering
+        for d in range(1, n_exp):
+            at = (d - 1) * PIECES + k
+            out = pltpu.make_async_remote_copy(
+                src_ref=out_ref.at[here], dst_ref=out_ref.at[here],
+                send_sem=ag_send.at[at], recv_sem=ag_recv.at[at],
+                device_id={"exp": peer(d)}, device_id_type=MESH,
+            )
+            out.start()
+            gather.append(out)
+    for k in range(PIECES):
+        for d in range(1, n_exp):
+            at = (d - 1) * PIECES + k
+            source = peer(n_exp - d)
+            pltpu.make_async_remote_copy(
+                src_ref=out_ref.at[block(source, k)], dst_ref=out_ref.at[block(source, k)],
+                send_sem=ag_send.at[at], recv_sem=ag_recv.at[at],
+                device_id={"exp": source}, device_id_type=MESH,
+            ).wait_recv()
     finish(first)
     finish(second)
-    for out in scatter + gather:
+    for out in list(scatter.values()) + gather:
         out.wait_send()
 
 
@@ -374,11 +384,11 @@
         pltpu.VMEM((2, 4, radius * radius // LANES, LANES), f32),
         pltpu.VMEM((tile, 2 * wide), f32),
         pltpu.VMEM((tile, tile), f32),
-        pltpu.VMEM((max(n_exp - 1, 1), tile // n_exp, tile), f32),
+        pltpu.VMEM((max(n_exp - 1, 1) * PIECES, tile // n_exp // PIECES, tile), f32),
         pltpu.SemaphoreType.DMA((len(tables) + 3,)),
         pltpu.SemaphoreType.DMA((2, len(DIRS))),
         pltpu.SemaphoreType.DMA((2, len(DIRS))),
-    ] + [pltpu.SemaphoreType.DMA((max(n_exp - 1, 1),))] * 4
+    ] + [pltpu.SemaphoreType.DMA((max(n_exp - 1, 1) * PIECES,))] * 4
     return pl.pallas_call(
         functools.partial(kernel, (n_exp, n_x, n_y, radius)),
         out_shape=jax.ShapeDtypeStruct((tile, tile), f32),

time: 34.1 us -> 34.7 us (1.018)
  Pallas kernels: 32.3 us -> 32.9 us
    pallas_call x1, Pallas kernels: 32.3 us -> 32.9 us  [shards(): pl.pallas_call(functools.partial(kernel, (n_exp, n_x, n_y, radius)), out_...]
where the time goes in v2:
time: 34.7 us; the launch traced here: 34.5 us
  Pallas kernels  32.9 us (95%)
  local copies, waits for them, and re-layouts  1.67 us (5%)
    pallas_call x1, Pallas kernels, shards(): pl.pallas_call(functools.partial(kernel, (n_exp, n_x, n_y, radius)), out_...  32.9 us
    unnamed x1, local copies, waits for them, and re-layouts  1.67 us

profile of v2, /device:TPU:0, one launch (start us, length us, event | category | flops | bytes accessed | tf_op | source)
XLA Modules:
  0.0 34.5 jit_solution(16786634346047817715)
XLA Ops:
  0.0 32.9 %shard_map.109 = f32[256,256]{1,0:T(8,128)} custom-call(f32[256,256]{1,0:T(8,128)} %h_est.1, f32[1,256,256]{2,1,0:T(8,128)} %h_obs.1, f32[1,65,4,65]{3,2,1,0:T(4,128)} %bitcast.1, s32[1,2,4]{2,1,0:T(2,128)} %idx_ref.1, s32[4,2,4]{2,1,0:T(2,128)} %cov_ref.1, bf16[2,384,512]{2,1,0:T(8,128)(2,1)} %constant.12.clone.h_fc, ...), custom_call_target="tpu_custom_call" | custom-call | tf_op jit(solution)/shard_map/pallas_call | solution.py:392
  32.9 1.7 %copy.13 = f32[256,256]{1,0:T(8,128)} copy(f32[256,256]{1,0:T(8,128)} %shard_map.109) | data formatting | bytes 524288
